TPU v7x, 128 devices: a whole 4x4x4 slice. The times are simulated.
128 devices in a mesh: row: 8 (over y, core), col: 16 (over z, x).
Axes of the slice: x: 4, y: 4, z: 4, core: 2. Of those that a mesh axis runs over, the one named last changes fastest.
Arguments:
- factor: float32 [256, 1536, 1536], P(('row', 'col'))
- coupling: bfloat16 [256, 1536, 512], P(('row', 'col')), may hold values from -0.15625 to 0.15625
- boundary: float32 [256, 512, 512], P(('row', 'col'))
- loads: float32 [32, 16384], P(None, ('row', 'col')), may hold values from -6 to 6
- block_ids: int32 [256, 16], P(('row', 'col')), may hold values from 0 to 511, as said below
- live_counts: int32 [256], P(('row', 'col')), may hold values from 8 to 16
Outputs:
- response: float32 [32, 16384], P(None, ('row', 'col'))
Inputs may be any that keep to these rules, and one draw needn't show every extreme that they name: `block_ids`: district d lies on device d // 2 (rows then columns of the mesh); its slot s names a block owned by the device in the same mesh row and in mesh column s % 16, where device p owns blocks p * 4 to p * 4 + 3.
All inputs are finite; a program needn't handle non-finite values.
Results may differ from a plain program's by a relative error of at most 0.0003.
Values sent between devices are 32-bit elements; how exact they have to be, the bound alone decides.
No kernel may reach another device: no remote copies, remote signals or barrier semaphores. Data moves between devices by JAX's collectives and lax.ppermute only.
A program may use at most 128 MiB of HBM per device.

v0:
```python
import jax
import jax.numpy as jnp
from jax import lax
from jax.sharding import PartitionSpec as P

BS = 32


def district_image(factor, coupling, boundary, picked, live_count):
    solved = jax.scipy.linalg.solve_triangular(factor, coupling.astype(jnp.float32), lower=True)
    schur_block = boundary - lax.dot_general(
        solved,
        solved,
        (((0,), (0,)), ((), ())),
        precision=lax.Precision.HIGHEST,
        preferred_element_type=jnp.float32,
    )
    weights = (jnp.arange(picked.shape[1]) < live_count).astype(jnp.float32)
    masked = (picked * weights[None, :, None]).reshape(picked.shape[0], -1)
    image = lax.dot_general(
        masked,
        schur_block,
        (((1,), (1,)), ((), ())),
        precision=lax.Precision.HIGHEST,
        preferred_element_type=jnp.float32,
    )
    return image.reshape(picked.shape) * weights[None, :, None]


def body(factor, coupling, boundary, loads, block_ids, live_counts):
    cases = loads.shape[0]
    gathered = lax.all_gather(loads, "col", axis=1, tiled=True)
    offset = lax.axis_index("row") * (gathered.shape[1] // BS)
    load_table = gathered.reshape(cases, -1, BS)
    images = []
    for district in range(factor.shape[0]):
        picked = jnp.take(load_table, block_ids[district] - offset, axis=1)
        images.append(
            district_image(
                factor[district],
                coupling[district],
                boundary[district],
                picked,
                live_counts[district],
            )
        )
    images = jnp.concatenate(images, axis=1)
    flat_ids = block_ids.reshape(-1)
    block_total = load_table.shape[1]
    onehot = ((flat_ids - offset)[:, None] == jnp.arange(block_total)[None, :]).astype(jnp.float32)
    dense_term = jnp.einsum("rsb,sj->rjb", images, onehot, precision=lax.Precision.HIGHEST).reshape(
        cases, -1
    )
    return lax.psum_scatter(dense_term, "col", scatter_dimension=1, tiled=True)


def solution(mesh):
    placed = (
        P(("row", "col"), None, None),
        P(("row", "col"), None, None),
        P(("row", "col"), None, None),
        P(None, ("row", "col")),
        P(("row", "col"), None),
        P(("row", "col")),
    )
    return jax.shard_map(
        body, mesh=mesh, in_specs=placed, out_specs=P(None, ("row", "col")), check_vma=False
    )
```

profile of v0, /device:TPU:0, one launch (start us, length us, event | category | flops | bytes accessed | tf_op | source)
XLA Modules:
  0.0 552.0 jit_solution(11103956469716437403)
XLA Ops:
  8.0 14.9 %bitcast_select_fusion.1 = (f32[1536,1536]{1,0:T(8,128)}, f32[1536,1536]{1,0:T(8,128)}) fusion(f32[2,1536,1536]{2,1,0:T(8,128)} %param.10), kind=kLoop, calls=%fused_computation.7 | loop fusion | flops 7077888 | bytes 37748736 | tf_op jit(solution)/shard_map/jit(_solve_triangular)/triangular_solve | solution.py:10
  23.9 40.8 %while.4 = (s32[]{:T(128)}, f32[1536,1536]{1,0:T(8,128)}, s32[12,2]{0,1:T(2,128)S(1)}, f32[12,128,128]{2,1,0:T(8,128)}, s32[]{:T(128)}) while((s32[]{:T(128)}, f32[1536,1536]{1,0:T(8,128)}, s32[12,2]{0,1:T(2,128)S(1)}, f32[12,128,128]{2,1,0:T(8,128)}, s32[]{:T(128)}) %tuple.167), condition=%wide.while_cond, body=%wide.while_body.sunk | while | flops 2 | bytes 132705 | solution.py:10
  24.5 2.8 bitcast_dynamic-update-slice_fusion.4
  27.9 2.8 bitcast_dynamic-update-slice_fusion.4
  31.3 2.8 bitcast_dynamic-update-slice_fusion.4
  34.7 2.8 bitcast_dynamic-update-slice_fusion.4
  38.1 2.8 bitcast_dynamic-update-slice_fusion.4
  41.5 2.8 bitcast_dynamic-update-slice_fusion.4
  44.9 2.8 bitcast_dynamic-update-slice_fusion.4
  48.3 2.8 bitcast_dynamic-update-slice_fusion.4
  51.8 2.8 bitcast_dynamic-update-slice_fusion.4
  55.2 2.8 bitcast_dynamic-update-slice_fusion.4
  58.6 2.8 bitcast_dynamic-update-slice_fusion.4
  62.0 2.8 bitcast_dynamic-update-slice_fusion.4
  64.7 119.5 %custom-call.4 = f32[12,128,128]{1,2,0:T(8,128)} custom-call(f32[12,128,128]{2,1,0:T(8,128)} %get-tuple-element.21), custom_call_target="InvertDiagBlocksLowerTriangular" | custom-call | tf_op jit(solution)/shard_map/jit(_solve_triangular)/triangular_solve | solution.py:10
  184.2 2.6 bitcast_convert_fusion.1
  189.2 1.3 convolution_subtract_fusion.12
  191.1 1.6 convolution_subtract_fusion.19
  193.2 1.7 convolution_subtract_fusion.23
  195.4 1.9 convolution_subtract_fusion.11
  197.8 2.0 convolution_subtract_fusion.18
  200.3 2.2 convolution_subtract_fusion.10
  203.0 2.3 convolution_subtract_fusion.9
  205.9 2.6 convolution_subtract_fusion.17
  208.9 3.1 convolution_subtract_fusion.22
  212.4 3.6 convolution_subtract_fusion.8
  216.0 25.4 %all_gather.3 = f32[32,2048]{1,0:T(8,128)S(1)} all-gather(f32[32,128]{1,0:T(8,128)S(1)} %copy-done.7), channel_id=1, replica_groups=mesh['row'=8,'col'=16] {'col'}, dimensions={1}, use_global_device_ids=true | all-gather | bytes 278528 | tf_op jit(solution)/shard_map/all_gather | solution.py:32
  241.4 1.3 reshape.71
  242.7 2.8 copy.7
  245.6 1.8 gather_fusion.1
  248.4 1.8 gather_fusion
  253.1 2.3 bitcast_multiply_fusion
  256.8 1.4 convolution_dynamic-update-slice_fusion.1
  258.2 6.4 %convolution_subtract_fusion.1 = f32[512,512]{1,0:T(8,128)S(1)} fusion(f32[1536,512]{1,0:T(8,128)S(1)} %convolution_dynamic-update-slice_fusion.1, f32[2,512,512]{2,1,0:T(8,128)} %param.12), kind=kOutput, calls=%fused_computation.12 | convolution fusion | flops 4832100352 | bytes 8388608 | tf_op jit(solution)/shard_map/dot_general | solution.py:11
  264.6 2.5 fusion.87
  268.1 1.9 broadcast_multiply_fusion.1
  271.0 42.2 %while.5 = (s32[]{:T(128)}, f32[1536,1536]{1,0:T(8,128)}, s32[12,2]{0,1:T(2,128)S(1)}, f32[12,128,128]{2,1,0:T(8,128)}, s32[]{:T(128)}) while((s32[]{:T(128)}, f32[1536,1536]{1,0:T(8,128)}, s32[12,2]{0,1:T(2,128)S(1)}, f32[12,128,128]{2,1,0:T(8,128)}, s32[]{:T(128)}) %tuple.172), condition=%wide.while_cond.clone, body=%wide.while_body.clone.sunk | while | flops 2 | bytes 132705 | solution.py:10
  271.6 2.9 bitcast_dynamic-update-slice_fusion.5
  275.1 2.9 bitcast_dynamic-update-slice_fusion.5
  278.7 2.9 bitcast_dynamic-update-slice_fusion.5
  282.2 2.9 bitcast_dynamic-update-slice_fusion.5
  285.7 2.9 bitcast_dynamic-update-slice_fusion.5
  289.2 2.9 bitcast_dynamic-update-slice_fusion.5
  292.7 2.9 bitcast_dynamic-update-slice_fusion.5
  296.3 2.9 bitcast_dynamic-update-slice_fusion.5
  299.8 2.9 bitcast_dynamic-update-slice_fusion.5
  303.3 2.9 bitcast_dynamic-update-slice_fusion.5
  306.8 2.9 bitcast_dynamic-update-slice_fusion.5
  310.3 2.9 bitcast_dynamic-update-slice_fusion.5
  313.2 119.5 %custom-call.5 = f32[12,128,128]{1,2,0:T(8,128)} custom-call(f32[12,128,128]{2,1,0:T(8,128)} %get-tuple-element.22), custom_call_target="InvertDiagBlocksLowerTriangular" | custom-call | tf_op jit(solution)/shard_map/jit(_solve_triangular)/triangular_solve | solution.py:10
  432.7 1.4 constant_dynamic-update-slice_fusion.122
  435.9 1.3 convolution_subtract_fusion.6
  437.8 1.6 convolution_subtract_fusion.16
  439.9 1.7 convolution_subtract_fusion.21
  442.1 1.9 convolution_subtract_fusion.5
  444.5 2.0 convolution_subtract_fusion.15
  447.0 2.2 convolution_subtract_fusion.4
  449.8 2.3 convolution_subtract_fusion.3
  452.6 2.6 convolution_subtract_fusion.14
  455.6 2.9 convolution_subtract_fusion.20
  459.0 3.1 convolution_subtract_fusion.2
  462.5 5.4 convolution_subtract_fusion
  468.3 2.5 fusion.88
  473.3 71.6 %reduce-scatter.2.cloned.1.call-done = f32[32,128]{1,0:T(8,128)} async-done(((f32[32,2048]{1,0:T(8,128)}), f32[32,128]{1,0:T(8,128)}) %reduce-scatter.2.cloned.1.call-update) | async-done | bytes 16400 | tf_op jit(solution)/shard_map/reduce_scatter | solution.py:54
  (117 shorter events, 40.6 us)
Async XLA Ops:
  6.5 538.4 %reduce-scatter.2.cloned.1.call-start = ((), (), s32[]{:S(2)}) async-start(), calls=%async_computation.1 | async-start | bytes 278528 | tf_op jit(solution)/shard_map/reduce_scatter | solution.py:54
  8.0 176.2 %copy-start.1 = (bf16[2,1536,512]{2,1,0:T(8,128)(2,1)S(1)}, bf16[2,1536,512]{2,1,0:T(8,128)(2,1)}, u32[]{:S(2)}) copy-start(bf16[2,1536,512]{2,1,0:T(8,128)(2,1)} %param.11) | copy-start | bytes 9437188
  184.2 2.6 copy-start.5
  212.0 4.1 copy-start.7
  242.7 8.5 %copy-start.8 = (s32[2]{0:T(128)S(1)}, s32[2]{0:T(128)}, u32[]{:S(2)}) copy-start(s32[2]{0:T(128)} %param.15) | copy-start | bytes 28
  264.6 168.1 %copy-start = (f32[1536,512]{1,0:T(8,128)S(1)}, f32[1536,512]{1,0:T(8,128)}, u32[]{:S(2)}) copy-start(f32[1536,512]{1,0:T(8,128)} %get-tuple-element.50) | copy-start | bytes 9437188
  432.7 2.7 copy-start.6
  458.5 4.0 copy-start.4
  462.5 5.4 copy-start.2
  467.9 3.2 copy-start.3
Sparse Core Ops, SparseCore 0:
  473.5 71.3 reduce-scatter.1
where the time goes:
time: 557 us; the launch traced here: 552 us
  other arithmetic  264 us (47%)
  local copies, waits for them, and re-layouts  100 us (18%)
  matrix products  77.2 us (14%)
  waiting for transfers between devices  71.6 us (13%)
  blocking collectives  25.4 us (5%)
  between operations  14.2 us (3%)
    another operation x4, other arithmetic, district_image(): jax.scipy.linalg.solve_triangular(factor, coupling.astype(jnp.float32), l...  254 us
    another operation x75, local copies, waits for them, and re-layouts, district_image(): jax.scipy.linalg.solve_triangular(factor, coupling.astype(jnp.float32), l...  84.9 us
    reduce_scatter x1, waiting for transfers between devices, body(): return lax.psum_scatter(dense_term, 'col', scatter_dimension=1, tiled=True)  71.6 us
    another operation x46, matrix products, district_image(): jax.scipy.linalg.solve_triangular(factor, coupling.astype(jnp.float32), l...  60 us
    all_gather x1, blocking collectives, body(): gathered = lax.all_gather(loads, 'col', axis=1, tiled=True)  25.4 us
    dot_general x2, matrix products, district_image(): lax.dot_general(solved, solved, (((0,), (0,)), ((), ())), precision=lax.P...  11.8 us
  transfers between devices with their start and end apart: 1, of which 1 were waited for; matrix products, arithmetic and copies ran while one was open for 0% of the time, Pallas kernels for 0%

commit v1 on v0

--- a/solution.py
+++ b/solution.py
@@ -29,7 +29,9 @@
 
 def body(factor, coupling, boundary, loads, block_ids, live_counts):
     cases = loads.shape[0]
-    gathered = lax.all_gather(loads, "col", axis=1, tiled=True)
+    gathered = jnp.concatenate(
+        lax.all_to_all(jnp.stack([loads] * lax.axis_size("col")), "col", 0, 0), axis=1
+    )
     offset = lax.axis_index("row") * (gathered.shape[1] // BS)
     load_table = gathered.reshape(cases, -1, BS)
     images = []

time: 557 us -> 535 us (0.961)
  blocking collectives: 25.4 us -> 0 us
  starting transfers between devices: 0.01 us -> 8.05 us
    all_gather x1 -> x0, blocking collectives: 25.4 us -> none  [body(): gathered = lax.all_gather(loads, 'col', axis=1, tiled=True)]
    all_to_all x0 -> x1, starting transfers between devices: none -> 8.01 us  [body(): lax.all_to_all(jnp.stack([loads] * lax.axis_size('col')), 'col', 0, 0)]
  transfers between devices with their start and end apart: 1 -> 2, of which waited for: 1 -> 1; matrix products, arithmetic and copies ran while one was open for 0% -> 79% of each run, Pallas kernels for 0% -> 0%
where the time goes in v1:
time: 535 us; the launch traced here: 529 us
  other arithmetic  259 us (48%)
  local copies, waits for them, and re-layouts  97.2 us (18%)
  matrix products  76.6 us (14%)
  waiting for transfers between devices  74 us (14%)
  between operations  14.2 us (3%)
  starting transfers between devices  8.05 us (2%)
    another operation x4, other arithmetic, district_image(): jax.scipy.linalg.solve_triangular(factor, coupling.astype(jnp.float32), l...  254 us
    another operation x75, local copies, waits for them, and re-layouts, district_image(): jax.scipy.linalg.solve_triangular(factor, coupling.astype(jnp.float32), l...  86 us
    reduce_scatter x1, waiting for transfers between devices, body(): return lax.psum_scatter(dense_term, 'col', scatter_dimension=1, tiled=True)  74 us
    another operation x46, matrix products, district_image(): jax.scipy.linalg.solve_triangular(factor, coupling.astype(jnp.float32), l...  59.5 us
    dot_general x2, matrix products, district_image(): lax.dot_general(solved, solved, (((0,), (0,)), ((), ())), precision=lax.P...  11.8 us
  transfers between devices with their start and end apart: 2, of which 1 were waited for; matrix products, arithmetic and copies ran while one was open for 79% of the time, Pallas kernels for 0%

profile of v1, /device:TPU:0, one launch (start us, length us, event | category | flops | bytes accessed | tf_op | source)
XLA Modules:
  0.0 529.4 jit_solution(12180967756184603346)
XLA Ops:
  6.5 1.4 stack.2
  8.0 8.0 %all-to-all-start = ((f32[16,32,128]{2,1,0:T(8,128)}), f32[16,32,128]{2,1,0:T(8,128)}, u32[]{:S(2)}, u32[]{:S(2)}) async-start(f32[16,32,128]{2,1,0:T(8,128)} %stack.2), calls=%async_computation | async-start | bytes 524288 | tf_op jit(solution)/shard_map/all_to_all | solution.py:33
  17.5 14.9 %bitcast_select_fusion.1 = (f32[1536,1536]{1,0:T(8,128)}, f32[1536,1536]{1,0:T(8,128)}) fusion(f32[2,1536,1536]{2,1,0:T(8,128)} %param.10), kind=kLoop, calls=%fused_computation.7 | loop fusion | flops 7077888 | bytes 37748736 | tf_op jit(solution)/shard_map/jit(_solve_triangular)/triangular_solve | solution.py:10
  33.4 40.8 %while.4 = (s32[]{:T(128)}, f32[1536,1536]{1,0:T(8,128)}, s32[12,2]{0,1:T(2,128)S(1)}, f32[12,128,128]{2,1,0:T(8,128)}, s32[]{:T(128)}) while((s32[]{:T(128)}, f32[1536,1536]{1,0:T(8,128)}, s32[12,2]{0,1:T(2,128)S(1)}, f32[12,128,128]{2,1,0:T(8,128)}, s32[]{:T(128)}) %tuple.167), condition=%wide.while_cond, body=%wide.while_body.sunk | while | flops 2 | bytes 132705 | solution.py:10
  34.0 2.8 bitcast_dynamic-update-slice_fusion.4
  37.4 2.8 bitcast_dynamic-update-slice_fusion.4
  40.8 2.8 bitcast_dynamic-update-slice_fusion.4
  44.2 2.8 bitcast_dynamic-update-slice_fusion.4
  47.6 2.8 bitcast_dynamic-update-slice_fusion.4
  51.0 2.8 bitcast_dynamic-update-slice_fusion.4
  54.5 2.8 bitcast_dynamic-update-slice_fusion.4
  57.9 2.8 bitcast_dynamic-update-slice_fusion.4
  61.3 2.8 bitcast_dynamic-update-slice_fusion.4
  64.7 2.8 bitcast_dynamic-update-slice_fusion.4
  68.1 2.8 bitcast_dynamic-update-slice_fusion.4
  71.5 2.8 bitcast_dynamic-update-slice_fusion.4
  74.2 119.5 %custom-call.4 = f32[12,128,128]{1,2,0:T(8,128)} custom-call(f32[12,128,128]{2,1,0:T(8,128)} %get-tuple-element.21), custom_call_target="InvertDiagBlocksLowerTriangular" | custom-call | tf_op jit(solution)/shard_map/jit(_solve_triangular)/triangular_solve | solution.py:10
  193.8 2.6 bitcast_convert_fusion.1
  196.9 1.2 convolution_subtract_fusion.13
  198.7 1.3 convolution_subtract_fusion.12
  200.6 1.6 convolution_subtract_fusion.19
  202.7 1.7 convolution_subtract_fusion.23
  204.9 1.9 convolution_subtract_fusion.11
  207.3 2.0 convolution_subtract_fusion.18
  209.8 2.2 convolution_subtract_fusion.10
  212.6 2.3 convolution_subtract_fusion.9
  215.4 2.6 convolution_subtract_fusion.17
  218.4 3.1 convolution_subtract_fusion.22
  221.9 2.9 convolution_subtract_fusion.8
  227.0 43.3 %while.5 = (s32[]{:T(128)}, f32[1536,1536]{1,0:T(8,128)}, s32[12,2]{0,1:T(2,128)S(1)}, f32[12,128,128]{2,1,0:T(8,128)}, s32[]{:T(128)}) while((s32[]{:T(128)}, f32[1536,1536]{1,0:T(8,128)}, s32[12,2]{0,1:T(2,128)S(1)}, f32[12,128,128]{2,1,0:T(8,128)}, s32[]{:T(128)}) %tuple.172), condition=%wide.while_cond.clone, body=%wide.while_body.clone.sunk | while | flops 2 | bytes 132705 | solution.py:10
  227.7 2.9 bitcast_dynamic-update-slice_fusion.5
  231.3 2.9 bitcast_dynamic-update-slice_fusion.5
  234.9 2.9 bitcast_dynamic-update-slice_fusion.5
  238.5 3.0 bitcast_dynamic-update-slice_fusion.5
  242.2 2.9 bitcast_dynamic-update-slice_fusion.5
  245.8 2.9 bitcast_dynamic-update-slice_fusion.5
  249.4 3.0 bitcast_dynamic-update-slice_fusion.5
  253.0 2.9 bitcast_dynamic-update-slice_fusion.5
  256.6 2.9 bitcast_dynamic-update-slice_fusion.5
  260.2 2.9 bitcast_dynamic-update-slice_fusion.5
  263.8 2.9 bitcast_dynamic-update-slice_fusion.5
  267.4 2.9 bitcast_dynamic-update-slice_fusion.5
  270.3 119.3 %custom-call.5 = f32[12,128,128]{1,2,0:T(8,128)} custom-call(f32[12,128,128]{2,1,0:T(8,128)} %get-tuple-element.22), custom_call_target="InvertDiagBlocksLowerTriangular" | custom-call | tf_op jit(solution)/shard_map/jit(_solve_triangular)/triangular_solve | solution.py:10
  389.7 1.7 constant_dynamic-update-slice_fusion.122
  391.3 1.4 convolution_subtract_fusion.7
  393.3 1.3 convolution_subtract_fusion.6
  395.2 1.6 convolution_subtract_fusion.16
  397.3 1.7 convolution_subtract_fusion.21
  399.5 1.9 convolution_subtract_fusion.5
  401.9 2.0 convolution_subtract_fusion.15
  404.4 2.2 convolution_subtract_fusion.4
  407.2 2.3 convolution_subtract_fusion.3
  410.0 2.6 convolution_subtract_fusion.14
  413.0 2.8 convolution_subtract_fusion.20
  416.3 3.1 convolution_subtract_fusion.2
  419.4 1.3 convolution_dynamic-update-slice_fusion.1
  420.7 6.2 %convolution_subtract_fusion.1 = f32[512,512]{1,0:T(8,128)} fusion(f32[1536,512]{1,0:T(8,128)S(1)} %convolution_dynamic-update-slice_fusion.1, f32[2,512,512]{2,1,0:T(8,128)S(1)} %copy-done.3), kind=kOutput, calls=%fused_computation.12 | convolution fusion | flops 4832100352 | bytes 8388608 | tf_op jit(solution)/shard_map/dot_general | solution.py:11
  427.3 5.6 %convolution_subtract_fusion = f32[512,512]{1,0:T(8,128)S(1)} fusion(f32[1536,512]{1,0:T(8,128)S(1)} %convolution_dynamic-update-slice_fusion, f32[2,512,512]{2,1,0:T(8,128)S(1)} %copy-done.3), kind=kOutput, calls=%fused_computation.11 | convolution fusion | flops 4832100352 | bytes 8388608 | tf_op jit(solution)/shard_map/dot_general | solution.py:11
  435.0 1.6 copy.15
  436.6 1.8 gather_fusion
  438.4 1.8 gather_fusion.1
  440.9 2.5 convolution_multiply_fusion.1
  443.4 2.5 convolution_multiply_fusion
  448.3 74.0 %reduce-scatter.2.cloned.1.call-done = f32[32,128]{1,0:T(8,128)} async-done(((f32[32,2048]{1,0:T(8,128)}), f32[32,128]{1,0:T(8,128)}) %reduce-scatter.2.cloned.1.call-update) | async-done | bytes 16400 | tf_op jit(solution)/shard_map/reduce_scatter | solution.py:56
  (111 shorter events, 36.0 us)
Async XLA Ops:
  8.0 425.6 %all-to-all-start = ((f32[16,32,128]{2,1,0:T(8,128)}), f32[16,32,128]{2,1,0:T(8,128)}, u32[]{:S(2)}, u32[]{:S(2)}) async-start(f32[16,32,128]{2,1,0:T(8,128)} %stack.2), calls=%async_computation | async-start | bytes 524288 | tf_op jit(solution)/shard_map/all_to_all | solution.py:33
  16.0 506.3 %reduce-scatter.2.cloned.1.call-start = ((), (), s32[]{:S(2)}) async-start(), calls=%async_computation.2 | async-start | bytes 278528 | tf_op jit(solution)/shard_map/reduce_scatter | solution.py:56
  17.5 176.2 %copy-start.2 = (bf16[2,1536,512]{2,1,0:T(8,128)(2,1)S(1)}, bf16[2,1536,512]{2,1,0:T(8,128)(2,1)}, u32[]{:S(2)}) copy-start(bf16[2,1536,512]{2,1,0:T(8,128)(2,1)} %param.11) | copy-start | bytes 9437188
  193.8 2.6 copy-start.4
  221.5 3.4 copy-start.6
  389.7 3.0 copy-start.5
  389.7 3.6 copy-start
  415.8 4.8 copy-start.3
  435.0 5.9 %copy-start.1 = (f32[512,512]{1,0:T(8,128)S(1)}, f32[512,512]{1,0:T(8,128)}, u32[]{:S(2)}) copy-start(f32[512,512]{1,0:T(8,128)} %convolution_subtract_fusion.1) | copy-start | bytes 3145732
Sparse Core Ops, SparseCore 0:
  448.4 73.8 reduce-scatter.1
